TPU v7x, 32 devices: a whole 2x2x4 slice. The times are simulated.
32 devices in a mesh: req: 8 (over z, x), tp: 4 (over y, core).
Axes of the slice: x: 2, y: 2, z: 4, core: 2. Of those that a mesh axis runs over, the one named last changes fastest.
Arguments:
- queries: bfloat16 [2, 8, 32, 1536], P(None, 'req', None, 'tp')
- response_kv: bfloat16 [2, 8, 2, 32, 256], P(None, 'req'), may hold values from -6 to 6
- cache_kv: bfloat16 [2, 8, 2, 384, 256], P(None, 'req'), may hold values from -6 to 6
- residual: bfloat16 [2, 8, 32, 1536], P(None, 'req')
- out_proj: bfloat16 [2, 1536, 1536], P(None, 'tp'), may hold values from -0.5 to 0.5
- norm_gain: float32 [2, 1536], replicated, may hold values from 0.25 to 1.75
- lm_head: bfloat16 [2, 8192, 1536], P(None, 'req', 'tp')
- targets: int32 [8, 32], P(None, 'tp'), may hold values from 0 to 8191
- resp_lengths: int32 [8], replicated, may hold values from 1 to 32, 160 in all
- cache_lengths: int32 [8], P('req'), may hold values from 1 to 384, 1920 in all
- owner_slot: int32 [8], replicated, may hold values from 0 to 7, each once
- sink_count: int32 [1], replicated, may hold values from 1 to 95
- window_size: int32 [1], replicated, may hold values from 48 to 191
Outputs:
- token_logprobs: float32 [8, 32], P('req', 'tp')
- request_scores: float32 [8, 2], P('req')
Inputs may be any that keep to these rules, and one draw needn't show every extreme that they name: `resp_lengths`: live response slots are the first ones; all lengths sum to 160. `cache_lengths`: live cache slots are the first ones; all lengths sum to 1920. `owner_slot`: A permutation of the requests.
All inputs are finite; a program needn't handle non-finite values. No bound on the sum of `cache_lengths` on one device may be relied on, other than what follows from the above.
Results may differ from a plain program's by a relative error of at most 0.0014.
Values may be sent and summed in bfloat16 or wider, within the bound.
No kernel may reach another device: no remote copies, remote signals or barrier semaphores. Data moves between devices by JAX's collectives and lax.ppermute only.
A program may use at most 128 MiB of HBM per device.

v0:
```python
import jax
import jax.numpy as jnp
from jax import lax
from jax.sharding import PartitionSpec as P

HEADS = 12
HEAD = 128
KV_HEADS = 2
RESP = 32
CACHE = 384


def span_mask(lengths, sink_count, window_size):
    cache_pos = jnp.arange(CACHE, dtype=jnp.int32)
    slot_pos = jnp.arange(RESP, dtype=jnp.int32)
    req_count = lengths.shape[0]
    key_pos = jnp.concatenate([cache_pos[None, :], lengths[:, None] + slot_pos[None, :]], axis=1)
    key_live = jnp.concatenate(
        [cache_pos[None, :] < lengths[:, None], jnp.ones((req_count, RESP), jnp.bool_)], axis=1
    )
    query_pos = lengths[:, None] + slot_pos[None, :]
    earlier = key_pos[:, None, :] <= query_pos[:, :, None]
    inside = (key_pos[:, None, :] < sink_count[0]) | (
        query_pos[:, :, None] - key_pos[:, None, :] < window_size[0]
    )
    return key_live[:, None, :] & earlier & inside


def rms_norm(hidden, norm_gain):
    scale_inv = lax.rsqrt(jnp.mean(hidden * hidden, axis=-1, keepdims=True) + 1e-06)
    return (hidden * scale_inv * norm_gain[:, None, None, :]).astype(jnp.bfloat16)


def per_device(
    queries,
    response_kv,
    cache_kv,
    residual,
    out_proj,
    norm_gain,
    lm_head,
    targets,
    resp_lengths,
    cache_lengths,
    owner_slot,
    sink_count,
    window_size,
):
    tp_size = lax.axis_size("tp")
    tp_index = lax.axis_index("tp")
    req_index = lax.axis_index("req")
    local_reqs = queries.shape[1]
    local_heads = HEADS // tp_size
    group_size = HEADS // KV_HEADS
    kv_index = tp_index * local_heads // group_size
    quarter = RESP // tp_size
    cache_head = lax.dynamic_slice_in_dim(cache_kv, kv_index * HEAD, HEAD, axis=4)
    resp_head = lax.dynamic_slice_in_dim(response_kv, kv_index * HEAD, HEAD, axis=4)
    key_rows = jnp.concatenate([cache_head[:, :, 0], resp_head[:, :, 0]], axis=2)
    value_rows = jnp.concatenate([cache_head[:, :, 1], resp_head[:, :, 1]], axis=2)
    query_heads = queries.reshape(2, local_reqs, RESP, local_heads, HEAD)
    scores = jnp.einsum(
        "mrshd,mrkd->mrhsk", query_heads, key_rows, preferred_element_type=jnp.float32
    ) * HEAD ** (-0.5)
    allowed = span_mask(cache_lengths, sink_count, window_size)[None, :, None]
    masked = jnp.where(allowed, scores, -jnp.inf)
    row_peak = jnp.max(masked, axis=-1, keepdims=True)
    weights = jnp.exp(masked - row_peak)
    weights = (weights / jnp.sum(weights, axis=-1, keepdims=True)).astype(jnp.bfloat16)
    attended = jnp.einsum(
        "mrhsk,mrkd->mrshd", weights, value_rows, preferred_element_type=jnp.float32
    )
    attended = attended.astype(jnp.bfloat16).reshape(2, local_reqs, RESP, local_heads * HEAD)
    partial_value = jnp.einsum(
        "mrsf,mfd->mrsd", attended, out_proj, preferred_element_type=jnp.float32
    )
    start_slot = tp_index * quarter
    projected = lax.dynamic_slice_in_dim(lax.psum(partial_value, "tp"), start_slot, quarter, axis=2)
    own_residual = lax.dynamic_slice_in_dim(residual, start_slot, quarter, axis=2)
    hidden = own_residual.astype(jnp.float32) + projected
    normed = rms_norm(hidden, norm_gain)
    flat_rows = normed.reshape(2, local_reqs * quarter, normed.shape[3])
    full_head = lax.all_gather(lm_head, "tp", axis=2, tiled=True)
    vocab_rows = full_head.shape[1]
    vocab_start = req_index * vocab_rows
    flat_targets = targets.reshape(-1)
    total_rows = flat_targets.shape[0]
    requests = total_rows // quarter
    logits = jnp.einsum(
        "mnd,mvd->mnv",
        lax.all_gather(flat_rows, "req", axis=1, tiled=True),
        full_head,
        preferred_element_type=jnp.float32,
    )
    block_peak = jnp.max(logits, axis=-1)
    block_total = jnp.sum(jnp.exp(logits - block_peak[..., None]), axis=-1)
    wanted = flat_targets - vocab_start
    target_hits = jnp.arange(vocab_rows, dtype=jnp.int32)[None, None, :] == wanted[None, :, None]
    block_pick = jnp.sum(jnp.where(target_hits, logits, 0.0), axis=-1)
    peak_all = block_peak
    total_all = block_total
    picked_all = block_pick
    peak_all = peak_all.reshape(2, requests, quarter)
    total_all = total_all.reshape(2, requests, quarter)
    picked_all = picked_all.reshape(2, requests, quarter)
    row_order = (
        jnp.zeros((requests,), jnp.int32).at[owner_slot].set(jnp.arange(requests, dtype=jnp.int32))
    )
    owned_reqs = lax.dynamic_slice_in_dim(row_order, req_index * local_reqs, local_reqs)
    vocab_top = lax.pmax(peak_all, "req")
    exp_total, picked = lax.psum((total_all * jnp.exp(peak_all - vocab_top), picked_all), "req")
    logprob = (picked - (vocab_top + jnp.log(exp_total)))[:, owned_reqs]
    lengths_owned = resp_lengths[owned_reqs]
    live_slots = (start_slot + jnp.arange(quarter, dtype=jnp.int32))[None, :] < lengths_owned[
        :, None
    ]
    policy = jnp.where(live_slots, logprob[0], 0.0)
    log_ratio = jnp.where(live_slots, logprob[0] - logprob[1], 0.0)
    policy_total, ratio_total = lax.psum(
        (jnp.sum(policy, axis=1), jnp.sum(log_ratio, axis=1)), "tp"
    )
    counts = lengths_owned.astype(jnp.float32)
    request_scores = jnp.stack([policy_total / counts, ratio_total / counts], axis=1)
    return (policy, request_scores)


def solution(mesh):
    in_specs = (
        P(None, "req", None, "tp"),
        P(None, "req", None, None, None),
        P(None, "req", None, None, None),
        P(None, "req", None, None),
        P(None, "tp", None),
        P(),
        P(None, "req", "tp"),
        P(None, "tp"),
        P(),
        P("req"),
        P(),
        P(),
        P(),
    )
    out_specs = (P("req", "tp"), P("req", None))
    return jax.shard_map(
        per_device, mesh=mesh, in_specs=in_specs, out_specs=out_specs, check_vma=False
    )
```

profile of v0, /device:TPU:0, one launch (start us, length us, event | category | flops | bytes accessed | tf_op | source)
XLA Modules:
  0.0 176.2 jit_solution(2035077833508412110)
XLA Ops:
  7.2 0.0 copy-start
  7.2 0.0 all-reduce.5.cloned.1.call-start
  7.3 1.2 dynamic-slice_bitcast_fusion
  8.5 0.8 dynamic-slice_bitcast_fusion.2
  11.2 0.8 reshape.303
  12.1 0.1 fusion.12
  12.2 0.3 fusion.23
  12.5 0.2 fusion.5
  12.7 0.3 fusion.2
  13.0 0.1 reshape.305
  13.1 0.0 copy-done
  13.1 0.0 copy-start.3
  13.1 0.0 copy-start.4
  13.1 0.0 copy-start.5
  13.1 0.0 copy-start.1
  13.2 0.0 copy-start.2
  13.2 1.3 convolution_bitcast_fusion
  14.4 0.0 all-reduce.5.cloned.1.call-update
  14.5 0.0 all-gather.3.cloned.1.call-start
  14.5 0.7 all-gather.3.cloned.1.call-update
  15.2 0.0 copy-done.3
  15.3 0.1 sub.65
  15.3 0.0 copy-done.4
  15.3 0.6 scatter_custom_fusion
  16.0 0.6 dynamic_slice.15
  18.5 0.0 copy-done.5
  18.5 0.6 dynamic-slice.5
  19.8 0.1 iota_compare_fusion
  19.9 30.1 %all-reduce.5.cloned.1.call-done = f32[2,1,32,1536]{3,2,0,1:T(8,128)} async-done(((f32[2,1,32,1536]{3,2,0,1:T(8,128)}), f32[2,1,32,1536]{3,2,0,1:T(8,128)}) %all-reduce.5.cloned.1.call-update) | async-done | bytes 393232 | tf_op jit(solution)/shard_map/psum | solution.py:78
  49.9 0.0 copy-done.1
  49.9 1.0 multiply_reduce_fusion
  50.9 0.0 copy-done.2
  50.9 1.0 multiply_convert_fusion
  51.9 31.4 %all-gather = bf16[2,1,64,1536]{3,2,0,1:T(8,128)(2,1)S(1)} all-gather(bf16[2,1,8,1536]{3,2,0,1:T(8,128)(2,1)S(1)} %multiply_convert_fusion), channel_id=2, replica_groups=mesh['req'=8,'tp'=4] {'req'}, dimensions={2}, use_global_device_ids=true | all-gather | bytes 442368 | tf_op jit(solution)/shard_map/all_gather | solution.py:91
  83.3 14.6 %all-gather.3.cloned.1.call-done = bf16[2,1024,1536]{2,1,0:T(8,128)(2,1)} async-done(((bf16[2,1024,384]{2,1,0:T(8,128)(2,1)}), bf16[2,1024,1536]{2,1,0:T(8,128)(2,1)}) %all-gather.3.cloned.1.call-update) | async-done | bytes 6291472 | tf_op jit(solution)/shard_map/all_gather | solution.py:83
  97.9 4.9 %fusion.24 = (f32[2,64]{1,0:T(2,128)S(1)}, f32[2,64,1024]{2,1,0:T(8,128)S(1)}) fusion(bf16[2,1024,1536]{2,1,0:T(8,128)(2,1)} %all-gather.3.cloned.1.call-done, bf16[2,1,64,1536]{3,2,0,1:T(8,128)(2,1)S(1)} %all-gather), kind=kOutput, calls=%fused_computation.60 | convolution fusion | flops 402784128 | bytes 7209472 | tf_op jit(solution)/shard_map/mnd,mvd->mnv/dot_general | solution.py:89
  102.8 0.1 reshape.308
  102.8 0.2 exponential_reduce_fusion
  103.1 0.1 reshape.309
  103.2 21.6 %pmax.7 = f32[2,8,8]{2,1,0:T(8,128)S(1)} all-reduce(f32[2,8,8]{2,1,0:T(8,128)S(1)} %reshape.308), channel_id=1, replica_groups=mesh['req'=8,'tp'=4] {'req'}, use_global_device_ids=true, to_apply=%region_8.9 | all-reduce | flops 128 | bytes 1024 | tf_op jit(solution)/shard_map/pmax | solution.py:110
  124.8 0.1 reshape.307
  124.9 33.0 %all-reduce.1 = (f32[2,8,8]{2,1,0:T(8,128)S(1)}, f32[2,8,8]{2,1,0:T(8,128)S(1)}) all-reduce(f32[2,8,8]{2,1,0:T(8,128)S(1)} %reshape.307, f32[2,8,8]{2,1,0:T(8,128)S(1)} %exponential_multiply_fusion), channel_id=1, replica_groups=mesh['req'=8,'tp'=4] {'req'}, use_global_device_ids=true, to_apply=%region_6.7 | all-reduce | flops 256 | bytes 2048 | tf_op jit(solution)/shard_map/psum | solution.py:111
  157.9 1.2 fusion.17
  159.1 1.7 fusion.22
  160.8 6.6 %all-reduce.2 = (f32[1]{0:T(128)}, f32[1]{0:T(128)}) all-reduce(f32[1]{0:T(128)} %bitcast.29, f32[1]{0:T(128)} %bitcast.26), channel_id=1, replica_groups=mesh['req'=8,'tp'=4] {'tp'}, use_global_device_ids=true, to_apply=%region_14.15 | all-reduce | flops 2 | bytes 16 | tf_op jit(solution)/shard_map/psum | solution.py:119
  168.8 0.6 pad_maximum_fusion
  (14 shorter events, 0.1 us)
Async XLA Ops:
  7.2 5.9 %copy-start = (bf16[2,384,1536]{2,1,0:T(8,128)(2,1)S(1)}, bf16[2,384,1536]{2,1,0:T(8,128)(2,1)}, u32[]{:S(2)}) copy-start(bf16[2,384,1536]{2,1,0:T(8,128)(2,1)} %param.17) | copy-start | bytes 7077892
  7.2 42.7 %all-reduce.5.cloned.1.call-start = ((), (), s32[]{:S(2)}) async-start(), calls=%async_computation | async-start | bytes 786432 | tf_op jit(solution)/shard_map/psum | solution.py:78
  13.1 2.1 %copy-start.3 = (s32[8,8]{1,0:T(8,128)S(1)}, s32[8,8]{1,0:T(8,128)}, u32[]{:S(2)}) copy-start(s32[8,8]{1,0:T(8,128)} %param.20) | copy-start | bytes 772
  13.1 2.2 %copy-start.4 = (s32[8]{0:T(128)S(1)}, s32[8]{0:T(128)}, u32[]{:S(2)}) copy-start(s32[8]{0:T(128)} %param.23) | copy-start | bytes 100
  13.1 5.4 %copy-start.5 = (s32[8]{0:T(128)S(1)}, s32[8]{0:T(128)}, u32[]{:S(2)}) copy-start(s32[8]{0:T(128)} %param.21) | copy-start | bytes 100
  13.1 36.8 %copy-start.1 = (bf16[2,1,32,1536]{3,2,1,0:T(8,128)(2,1)S(1)}, bf16[2,1,32,1536]{3,2,1,0:T(8,128)(2,1)}, u32[]{:S(2)}) copy-start(bf16[2,1,32,1536]{3,2,1,0:T(8,128)(2,1)} %param.16) | copy-start | bytes 589828
  13.2 37.8 %copy-start.2 = (f32[2,1536]{1,0:T(2,128)S(1)}, f32[2,1536]{1,0:T(2,128)}, u32[]{:S(2)}) copy-start(f32[2,1536]{1,0:T(2,128)} %param.18) | copy-start | bytes 36868
  14.5 83.4 %all-gather.3.cloned.1.call-start = ((), (), s32[]{:S(2)}) async-start(), calls=%async_computation.1 | async-start | bytes 7864320 | tf_op jit(solution)/shard_map/all_gather | solution.py:83
Sparse Core Ops, SparseCore 0:
  14.6 35.2 all-reduce.4
  51.6 46.2 all-gather.2
where the time goes:
time: 177 us; the launch traced here: 176 us
  blocking collectives  92.6 us (52%)
  waiting for transfers between devices  45.3 us (26%)
  between operations  20.2 us (11%)
  matrix products  6.74 us (4%)
  other arithmetic  6.26 us (4%)
  local copies, waits for them, and re-layouts  5.05 us (3%)
    psum x1, blocking collectives, per_device(): lax.psum((total_all * jnp.exp(peak_all - vocab_top), picked_all), 'req')  33 us
    all_gather x1, blocking collectives, per_device(): lax.all_gather(flat_rows, 'req', axis=1, tiled=True)  31.4 us
    psum x1, waiting for transfers between devices, per_device(): lax.psum(partial_value, 'tp')  30.1 us
    pmax x1, blocking collectives, per_device(): vocab_top = lax.pmax(peak_all, 'req')  21.6 us
    all_gather x1, waiting for transfers between devices, per_device(): full_head = lax.all_gather(lm_head, 'tp', axis=2, tiled=True)  14.6 us
    psum x1, blocking collectives, per_device(): lax.psum((jnp.sum(policy, axis=1), jnp.sum(log_ratio, axis=1)), 'tp')  6.62 us
    dot_general x1, matrix products, per_device(): jnp.einsum('mnd,mvd->mnv', lax.all_gather(flat_rows, 'req', axis=1, tiled...  4.87 us
  transfers between devices with their start and end apart: 2, of which 2 were waited for; matrix products, arithmetic and copies ran while one was open for 2% of the time, Pallas kernels for 0%

commit v1 on v0

v1 whole, which is shorter than its diff:
```python
import functools

import jax
import jax.numpy as jnp
from jax import lax
from jax.experimental import pallas as pl
from jax.experimental.pallas import tpu as pltpu
from jax.sharding import PartitionSpec as P

HEADS = 12
HEAD = 128
KV_HEADS = 2
RESP = 32
CACHE = 384
LANES = 128
MIB = 1 << 20
BRIEF = pl.CostEstimate(flops=1, bytes_accessed=1, transcendentals=0)
VMEM = pl.BlockSpec(memory_space=pltpu.VMEM)
SMEM = pl.BlockSpec(memory_space=pltpu.SMEM)
HBM = pl.BlockSpec(memory_space=pltpu.HBM)


def swap(value, axis, distance):
    size = lax.axis_size(axis)
    return lax.ppermute(value, axis, [(i, i ^ distance) for i in range(size)])


def exchange_steps(size):
    bits = []
    while 2 ** len(bits) < size:
        bits.append(2 ** len(bits))
    groups = [bits[i : i + 2] for i in range(1, len(bits), 2)] + [bits[:1]]
    return [g if len(g) == 1 else [g[0] | g[1], g[1], g[0]] for g in groups]


def gather_order(size):
    order = [0]
    for steps in exchange_steps(size):
        order = order + [step ^ k for step in steps for k in order]
    return order


def offsets_of(lengths, requests):
    starts, running = [], jnp.int32(0)
    for i in range(requests):
        starts.append(running)
        running = running + lengths[i]
    return starts


def attend_kernel(
    tp_size,
    order,
    cache_len,
    sink,
    window,
    lengths_ref,
    owners_ref,
    q_ref,
    targets_ref,
    residual_ref,
    gain_ref,
    resp_ref,
    cache_ref,
    proj_ref,
    send_ref,
    keep_ref,
    own_gain_ref,
    index_ref,
    code_ref,
    span_ref,
    lengths,
    owners,
    q_buf,
    targets_buf,
    residual_buf,
    gain_buf,
    resp_buf,
    cache_buf,
    proj_buf,
    sems,
):
    tp_index = lax.axis_index("tp")
    req_index = lax.axis_index("req")
    requests = len(order)
    heads = HEADS // tp_size
    chunk = proj_ref.shape[2] // tp_size
    quarter = RESP // tp_size
    kv_lane = pl.multiple_of(tp_index * heads // (HEADS // KV_HEADS) * HEAD, HEAD)
    model = tp_index % 2
    own_lane = pl.multiple_of(tp_index // 2 * 2 * chunk, LANES)
    rows_each = proj_ref.shape[1] // 1
    pairs = [
        (cache_ref.at[:, 0, :, :, pl.ds(kv_lane, HEAD)], cache_buf),
        (q_ref.at[:, 0], q_buf),
        (resp_ref.at[:, 0, :, :, pl.ds(kv_lane, HEAD)], resp_buf),
        (residual_ref.at[model, 0, :, pl.ds(own_lane, 2 * chunk)], residual_buf),
        (gain_ref.at[pl.ds(model, 1), pl.ds(own_lane, 2 * chunk)], gain_buf),
        (targets_ref, targets_buf),
        (lengths_ref, lengths),
        (owners_ref, owners),
    ] + [
        (proj_ref.at[m, pl.ds(i * rows_each, rows_each)], proj_buf.at[m, pl.ds(i * rows_each, rows_each)])
        for m in range(2)
        for i in range(1)
    ]
    copies = [
        pltpu.make_async_copy(source, target, sems.at[i])
        for i, (source, target) in enumerate(pairs)
    ]
    for copy in copies:
        copy.start()
    for copy in copies[:3]:
        copy.wait()
    length = cache_len[0]
    rows = heads * RESP
    slot = lax.broadcasted_iota(jnp.int32, (rows, CACHE), 0) % RESP
    key = lax.broadcasted_iota(jnp.int32, (rows, CACHE), 1)
    cache_ok = (key < length) & ((key < sink[0]) | (length + slot - key < window[0]))
    slot = lax.broadcasted_iota(jnp.int32, (rows, RESP), 0) % RESP
    key = lax.broadcasted_iota(jnp.int32, (rows, RESP), 1)
    resp_ok = (key <= slot) & ((length + key < sink[0]) | (slot - key < window[0]))
    contract_last = (((1,), (1,)), ((), ()))
    attended = []
    for m in range(2):
        q = jnp.concatenate([q_buf[m, :, h * HEAD : (h + 1) * HEAD] for h in range(heads)], axis=0)
        cache_score = lax.dot_general(
            q, cache_buf[m, 0], contract_last, preferred_element_type=jnp.float32
        ) * HEAD ** (-0.5)
        resp_score = lax.dot_general(
            q, resp_buf[m, 0], contract_last, preferred_element_type=jnp.float32
        ) * HEAD ** (-0.5)
        cache_score = jnp.where(cache_ok, cache_score, -jnp.inf)
        resp_score = jnp.where(resp_ok, resp_score, -jnp.inf)
        peak = jnp.maximum(
            jnp.max(cache_score, axis=1, keepdims=True), jnp.max(resp_score, axis=1, keepdims=True)
        )
        cache_exp = jnp.exp(cache_score - peak)
        resp_exp = jnp.exp(resp_score - peak)
        total = jnp.sum(cache_exp, axis=1, keepdims=True) + jnp.sum(resp_exp, axis=1, keepdims=True)
        out = jnp.dot(
            (cache_exp / total).astype(jnp.bfloat16), cache_buf[m, 1], preferred_element_type=jnp.float32
        ) + jnp.dot(
            (resp_exp / total).astype(jnp.bfloat16), resp_buf[m, 1], preferred_element_type=jnp.float32
        )
        out = out.astype(jnp.bfloat16)
        attended.append(
            jnp.concatenate([out[h * RESP : (h + 1) * RESP] for h in range(heads)], axis=1)
        )
    for copy in copies[3:]:
        copy.wait()
    own = jnp.where(model == 0, attended[0], attended[1])
    other = jnp.where(model == 0, attended[1], attended[0])
    for k in range(tp_size):
        columns = slice(k * chunk, (k + 1) * chunk)
        for target, rows, m, t in (
            (send_ref, other, 1 - model, tp_index ^ 1 ^ k),
            (keep_ref, own, model, tp_index ^ k),
        ):
            weights = proj_buf[m, :, pl.ds(pl.multiple_of(t * chunk, LANES), chunk)]
            target[0:RESP, columns] = jnp.dot(rows, weights, preferred_element_type=jnp.float32)
    for k in range(2):
        lanes = pl.ds(pl.multiple_of((model ^ k) * chunk, LANES), chunk)
        columns = slice(k * chunk, (k + 1) * chunk)
        keep_ref[0:RESP, columns] += residual_buf[:, lanes].astype(jnp.float32)
        own_gain_ref[:, columns] = gain_buf[:, lanes]
    own_targets = targets_buf[...]
    place = lax.broadcasted_iota(jnp.int32, (quarter, LANES), 1) - tp_index * quarter
    spread = (place == lax.broadcasted_iota(jnp.int32, (quarter, LANES), 0)).astype(jnp.float32)
    for target in (send_ref, keep_ref):
        target[RESP:, :] = jnp.zeros((requests, tp_size * chunk), jnp.float32)
    for digit in range(3):
        value = ((own_targets >> (8 * digit)) & 255).astype(jnp.float32)
        value = jnp.dot(value, spread, preferred_element_type=jnp.float32)
        lanes = slice(2 * chunk + digit * LANES, 2 * chunk + (digit + 1) * LANES)
        for target in (send_ref, keep_ref):
            target[RESP:, lanes] = value
    starts = offsets_of(lengths, requests)
    column = lax.broadcasted_iota(jnp.int32, index_ref.shape, 1)
    source = jnp.zeros(index_ref.shape, jnp.int32)
    for at, k in enumerate(order):
        source = jnp.where(column // RESP == at, req_index ^ k, source)
    base = jnp.zeros(index_ref.shape, jnp.int32)
    count = jnp.zeros(index_ref.shape, jnp.int32)
    per_device = code_ref.shape[0]
    row = tp_index // 2 * per_device + lax.broadcasted_iota(jnp.int32, code_ref.shape, 0)
    code = jnp.zeros(code_ref.shape, jnp.int32)
    own_start, own_count = jnp.int32(0), jnp.int32(1)
    for i in range(requests):
        base = jnp.where(source == i, starts[i], base)
        count = jnp.where(source == i, lengths[i], count)
        code = jnp.where(row >= starts[i], row - starts[i] + i * RESP, code)
        own_start = jnp.where(owners[i] == req_index, starts[i], own_start)
        own_count = jnp.where(owners[i] == req_index, lengths[i], own_count)
    index_ref[...] = jnp.where(column % RESP < count, base + column % RESP, -1)
    code_ref[...] = code
    lane = lax.broadcasted_iota(jnp.int32, span_ref.shape, 1)
    span_ref[...] = jnp.where(lane == 0, own_start, own_count)


def logits_kernel(tp_size, block, index_ref, rows_ref, gain_ref, head_ref, got_ref, sent_ref, keep_ref):
    tp_index = lax.axis_index("tp")
    step = pl.program_id(0)
    wide = index_ref.shape[1]
    total = tp_size * block
    per_block = wide * 5 // 8 // tp_size
    pair = tp_index // 2
    row = lax.broadcasted_iota(jnp.int32, (total, 1), 0)
    wanted = jnp.zeros((total, 1), jnp.int32)
    for place in range(tp_size):
        first = (2 * (pair ^ (1 - place // 2)) + place % 2) * per_block + step * block - place * block
        wanted = jnp.where(row // block == place, row + first, wanted)
    pick = (wanted == index_ref[...]).astype(jnp.float32).astype(jnp.bfloat16)
    vocab, chunk = got_ref.shape
    rows = rows_ref[...].reshape(wide, 2 * chunk)
    live = jnp.dot(pick, rows, preferred_element_type=jnp.float32)
    bare = live * (1.0 / gain_ref[...])
    square = jnp.broadcast_to(jnp.sum(bare * bare, axis=1, keepdims=True), (total, LANES))
    live = live.astype(jnp.bfloat16)
    contract_last = (((1,), (1,)), ((), ()))
    head = jnp.concatenate([head_ref[tp_index % 2], got_ref[...]], axis=1)
    logits = lax.dot_general(live, head, contract_last, preferred_element_type=jnp.float32)
    lane = lax.broadcasted_iota(jnp.int32, (block, LANES), 1)
    for place in range(tp_size):
        span = slice(place * block, (place + 1) * block)
        body, whole = logits[span], square[span]
        if place // 2:
            keep_ref[place % 2, :, 0:vocab] = body
            keep_ref[place % 2, :, vocab : vocab + LANES] = whole
            continue
        coarse = body.astype(jnp.bfloat16).astype(jnp.float32)
        size = jnp.abs(body)
        top = jnp.max(size, axis=1, keepdims=True)
        rest = jnp.max(jnp.where(size == top, body - coarse, -jnp.inf), axis=1, keepdims=True)
        high = whole.astype(jnp.bfloat16).astype(jnp.float32)
        tail = jnp.where(lane == 0, high, whole - high)
        tail = jnp.where(lane == 2, rest, tail)
        tail = jnp.where(lane == 3, top, tail)
        sent_ref[place % 2, :, 0:vocab] = coarse
        sent_ref[place % 2, :, vocab : vocab + LANES] = tail


def lse_kernel(m, width, keep_ref, last_ref, targets_ref, code_ref, *refs):
    stats_ref = refs[-1]
    req_index = lax.axis_index("req")
    block = code_ref.shape[0]
    vocab = keep_ref.shape[2] - LANES
    requests = targets_ref.shape[0]
    code = code_ref[...]
    lane = lax.broadcasted_iota(jnp.int32, (block, LANES), 1)
    digits = jnp.zeros((block, LANES), jnp.float32)
    for i in range(requests):
        here = (
            targets_ref[i : i + 1, 0:LANES]
            + targets_ref[i : i + 1, LANES : 2 * LANES] * 256.0
            + targets_ref[i : i + 1, 2 * LANES : 3 * LANES] * 65536.0
        )
        digits = digits + jnp.where(code == i * RESP + lane, jnp.where(lane < RESP, here, 0.0), 0.0)
    wanted = jnp.sum(digits, axis=1, keepdims=True).astype(jnp.int32) - req_index * vocab
    near = keep_ref[0]
    tail = last_ref[:, vocab : vocab + LANES]
    column = lax.broadcasted_iota(jnp.int32, (block, vocab), 1)
    last = last_ref[:, 0:vocab]
    logits = near[:, 0:vocab] + last + jnp.where(jnp.abs(last) == tail[:, 3:4], tail[:, 2:3], 0.0)
    square = near[:, vocab : vocab + 1] + tail[:, 0:1] + tail[:, 1:2]
    logits = logits * lax.rsqrt(square / width + 1e-06)
    peak = jnp.max(logits, axis=1, keepdims=True)
    lse = peak + jnp.log(jnp.sum(jnp.exp(logits - peak), axis=1, keepdims=True))
    picked = jnp.sum(jnp.where(column == wanted, logits, 0.0), axis=1, keepdims=True)
    stats = jnp.where(lane == 0, lse, jnp.where(lane == 1, picked, 0.0))
    if m:
        space = jnp.zeros((LANES // 2 - block, LANES), jnp.float32)
        stats = jnp.concatenate([refs[0][...], space, stats, space], axis=0)
        stats = jnp.broadcast_to(stats.T[0:2], stats_ref.shape)
    stats_ref[...] = stats


def final_kernel(tp_size, block, per_device, span_ref, stats_ref, policy_ref, scores_ref):
    tp_index = lax.axis_index("tp")
    step = pl.program_id(0)
    quarter = policy_ref.shape[1]
    stats = stats_ref[...].reshape((-1, tp_size) + stats_ref.shape[1:])
    peak = jnp.max(stats[:, :, 0:1], axis=0)
    whole = peak + jnp.log(jnp.sum(jnp.exp(stats[:, :, 0:1] - peak), axis=0))
    logprob = jnp.sum(stats[:, :, 1:2], axis=0) - whole
    start = span_ref[0:1, 0:1]
    count = span_ref[0:1, 1:2]
    lane = lax.broadcasted_iota(jnp.int32, (1, LANES), 1)
    inner = lane % (LANES // 2)
    own = tp_index * quarter + lax.broadcasted_iota(jnp.int32, (quarter, 1), 0)
    policy = jnp.zeros((quarter, 1), jnp.float32)
    total = jnp.zeros((1, 1), jnp.float32)
    ratio = jnp.zeros((1, 1), jnp.float32)
    part = jnp.where(lane < LANES // 2, 0, 1)
    for t in range(tp_size):
        slot = (t // 2 * 2 + part) * per_device + step * block + inner - start
        live = (inner < block) & (slot >= 0) & (slot < count)
        value = jnp.where(live, logprob[t], 0.0)
        if t % 2:
            ratio = ratio - jnp.sum(value, axis=1, keepdims=True)
        else:
            policy = policy + jnp.sum(
                jnp.where(live & (slot == own), value, 0.0), axis=1, keepdims=True
            )
            total = total + jnp.sum(value, axis=1, keepdims=True)
            ratio = ratio + jnp.sum(value, axis=1, keepdims=True)
    eye = lax.broadcasted_iota(jnp.int32, (quarter, quarter), 0) == lax.broadcasted_iota(
        jnp.int32, (quarter, quarter), 1
    )
    policy = jnp.sum(jnp.where(eye, policy, 0.0), axis=0, keepdims=True)
    divisor = count.astype(jnp.float32)
    lane = lax.broadcasted_iota(jnp.int32, (1, 2), 1)
    scores = jnp.where(lane == 0, total / divisor, ratio / divisor)

    @pl.when(step == 0)
    def _():
        policy_ref[...] = policy
        scores_ref[...] = scores

    @pl.when(step > 0)
    def _():
        policy_ref[...] += policy
        scores_ref[...] += scores


def per_device(
    queries,
    response_kv,
    cache_kv,
    residual,
    out_proj,
    norm_gain,
    lm_head,
    targets,
    resp_lengths,
    cache_lengths,
    owner_slot,
    sink_count,
    window_size,
):
    tp_size = lax.axis_size("tp")
    requests = targets.shape[0]
    quarter = RESP // tp_size
    width = residual.shape[3]
    chunk = width // tp_size
    per_block = requests * RESP * 5 // 8 // tp_size
    f32, bf16, i32 = jnp.float32, jnp.bfloat16, jnp.int32
    order = gather_order(lax.axis_size("req"))
    packed = jax.ShapeDtypeStruct((RESP + requests, width), f32)
    send, keep, own_gain, index, code, span = pl.pallas_call(
        functools.partial(attend_kernel, tp_size, order),
        out_shape=(
            packed,
            packed,
            jax.ShapeDtypeStruct((1, 2 * chunk), f32),
            jax.ShapeDtypeStruct((1, requests * RESP), i32),
            jax.ShapeDtypeStruct((2 * per_block, LANES), i32),
            jax.ShapeDtypeStruct((1, LANES), i32),
        ),
        in_specs=[SMEM] * 3 + [HBM] * 9,
        out_specs=(VMEM,) * 6,
        scratch_shapes=[
            pltpu.SMEM((requests,), i32),
            pltpu.SMEM((requests,), i32),
            pltpu.VMEM((2, RESP, queries.shape[3]), bf16),
            pltpu.VMEM(targets.shape, i32),
            pltpu.VMEM((RESP, 2 * chunk), bf16),
            pltpu.VMEM((1, 2 * chunk), f32),
            pltpu.VMEM((2, 2, RESP, HEAD), bf16),
            pltpu.VMEM((2, 2, CACHE, HEAD), bf16),
            pltpu.VMEM(out_proj.shape, bf16),
            pltpu.SemaphoreType.DMA((8 + 2,)),
        ],
        compiler_params=pltpu.CompilerParams(vmem_limit_bytes=16 * MIB),
        name="attend",
    )(
        cache_lengths,
        sink_count,
        window_size,
        *[
            pltpu.with_memory_space_constraint(operand, pltpu.HBM)
            for operand in (
                resp_lengths,
                owner_slot,
                queries,
                targets,
                residual,
                norm_gain,
                response_kv,
                cache_kv,
                out_proj,
            )
        ]
    )
    head, send = lax.optimization_barrier((lm_head, send))
    head = lax.dynamic_index_in_dim(head, 1 - lax.axis_index("tp") % 2, axis=0, keepdims=False)
    head = swap(head, "tp", 1)
    whole = keep + swap(send.astype(bf16), "tp", 1).astype(f32)
    got = swap(whole[:, 2 * chunk :].astype(bf16), "tp", 2).astype(f32)
    riders = whole[RESP:, 2 * chunk : 2 * chunk + 3 * LANES] + got[RESP:, : 3 * LANES]
    scaled = ((whole[:RESP, : 2 * chunk] + got[:RESP]) * own_gain).astype(bf16)
    steps = max(1, requests // 8)
    block = per_block // steps
    vocab = lm_head.shape[1]
    flat = pl.BlockSpec((block, vocab + LANES), lambda g: (g, 0))
    slab = pl.BlockSpec((block, LANES), lambda g: (g, 0))
    rows = scaled[None]
    *groups, longest, _ = exchange_steps(lax.axis_size("req"))
    for group in groups:
        rows = jnp.concatenate([rows] + [swap(rows, "req", step) for step in group], axis=0)
    got = [swap(rows, "req", step) for step in longest]
    side = swap(rows, "req", 1)
    far = [swap(got[0], "req", 1), swap(jnp.concatenate(got[1:], axis=0), "req", 1)]
    rows = jnp.concatenate([rows] + got + [side] + far, axis=0)
    packed = jax.ShapeDtypeStruct((2, per_block, vocab + LANES), f32)
    spec = pl.BlockSpec((2, block, vocab + LANES), lambda g: (0, g, 0))
    sent, keep = pl.pallas_call(
        functools.partial(logits_kernel, tp_size, block),
        out_shape=(packed, packed),
        grid=(steps,),
        in_specs=[VMEM] * 5,
        out_specs=(spec, spec),
        compiler_params=pltpu.CompilerParams(vmem_limit_bytes=32 * MIB),
        cost_estimate=BRIEF,
        name="logits",
    )(index, rows, own_gain, lm_head, head)
    parts = [swap(sent[i].astype(bf16), "tp", 2).astype(f32) for i in range(2)]
    everyone = lax.axis_size("req") * tp_size
    wide = pl.BlockSpec((everyone, 2, LANES), lambda g: (0, 0, g))
    stats = []
    for m, last in enumerate(parts):
        shape = (everyone, 2, steps * LANES) if m else (per_block, LANES)
        stats = [
            pl.pallas_call(
                functools.partial(lse_kernel, m, width),
                out_shape=jax.ShapeDtypeStruct(shape, f32),
                grid=(steps,),
                in_specs=[
                    pl.BlockSpec((1, block, vocab + LANES), lambda g, m=m: (m, g, 0)),
                    flat,
                    VMEM,
                    pl.BlockSpec((block, LANES), lambda g, m=m: (m * steps + g, 0)),
                ]
                + [slab] * m,
                out_specs=wide if m else slab,
                compiler_params=pltpu.CompilerParams(vmem_limit_bytes=16 * MIB),
                cost_estimate=BRIEF,
                name="lse",
            )(keep, last, riders, code, *stats)
        ]
    stats = lax.all_to_all(stats[0], ("req", "tp"), 0, 0, tiled=True)
    return pl.pallas_call(
        functools.partial(final_kernel, tp_size, block, per_block),
        out_shape=(
            jax.ShapeDtypeStruct((1, quarter), f32),
            jax.ShapeDtypeStruct((1, 2), f32),
        ),
        grid=(steps,),
        in_specs=[VMEM, wide],
        out_specs=(VMEM, VMEM),
        compiler_params=pltpu.CompilerParams(vmem_limit_bytes=8 * MIB),
        name="final",
    )(span, stats)


def solution(mesh):
    in_specs = (
        P(None, "req", None, "tp"),
        P(None, "req", None, None, None),
        P(None, "req", None, None, None),
        P(None, "req", None, None),
        P(None, "tp", None),
        P(),
        P(None, "req", "tp"),
        P(None, "tp"),
        P(),
        P("req"),
        P(),
        P(),
        P(),
    )
    out_specs = (P("req", "tp"), P("req", None))
    return jax.shard_map(
        per_device, mesh=mesh, in_specs=in_specs, out_specs=out_specs, check_vma=False
    )
```

time: 177 us -> 45.7 us (0.26)
  blocking collectives: 92.6 us -> 8.94 us
  waiting for transfers between devices: 45.3 us -> 14.6 us
  between operations: 20.2 us -> 2.72 us
  starting transfers between devices: 0.08 us -> 14.1 us
  matrix products: 6.74 us -> 0 us
  other arithmetic: 6.26 us -> 0.16 us
  Pallas kernels: 0 us -> 4.93 us
  local copies, waits for them, and re-layouts: 5.05 us -> 0.14 us
    psum x2 -> x0, blocking collectives: 39.6 us -> none  [the longest x1 33 us: per_device(): lax.psum((total_all * jnp.exp(peak_all - vocab_top), picked_all), 'req')]
    all_gather x1 -> x0, blocking collectives: 31.4 us -> none  [per_device(): lax.all_gather(flat_rows, 'req', axis=1, tiled=True)]
    psum x1 -> x0, waiting for transfers between devices: 30.1 us -> none  [per_device(): lax.psum(partial_value, 'tp')]
    pmax x1 -> x0, blocking collectives: 21.6 us -> none  [per_device(): vocab_top = lax.pmax(peak_all, 'req')]
    all_gather x1 -> x0, waiting for transfers between devices: 14.6 us -> none  [per_device(): full_head = lax.all_gather(lm_head, 'tp', axis=2, tiled=True)]
    ppermute x0 -> x11, waiting for transfers between devices: none -> 14.6 us  [swap(): return lax.ppermute(value, axis, [(i, i ^ distance) for i in range(size)])]
    ppermute x0 -> x11, starting transfers between devices: none -> 14.1 us  [swap(): return lax.ppermute(value, axis, [(i, i ^ distance) for i in range(size)])]
    all_to_all x0 -> x1, blocking collectives: none -> 8.94 us  [per_device(): stats = lax.all_to_all(stats[0], ('req', 'tp'), 0, 0, tiled=True)]
  transfers between devices with their start and end apart: 2 -> 11, of which waited for: 2 -> 7; matrix products, arithmetic and copies ran while one was open for 2% -> 0% of each run, Pallas kernels for 0% -> 1%
where the time goes in v1:
time: 45.7 us; the launch traced here: 45.6 us
  waiting for transfers between devices  14.6 us (32%)
  starting transfers between devices  14.1 us (31%)
  blocking collectives  8.94 us (20%)
  Pallas kernels  4.93 us (11%)
  between operations  2.72 us (6%)
    ppermute x11, waiting for transfers between devices, swap(): return lax.ppermute(value, axis, [(i, i ^ distance) for i in range(size)])  14.6 us
    ppermute x11, starting transfers between devices, swap(): return lax.ppermute(value, axis, [(i, i ^ distance) for i in range(size)])  14.1 us
    all_to_all x1, blocking collectives, per_device(): stats = lax.all_to_all(stats[0], ('req', 'tp'), 0, 0, tiled=True)  8.94 us
    pallas_call x1, Pallas kernels, per_device(): pl.pallas_call(functools.partial(attend_kernel, tp_size, order), out_shap...  2.54 us
    pallas_call x1, Pallas kernels, per_device(): pl.pallas_call(functools.partial(logits_kernel, tp_size, block), out_shap...  0.92 us
  transfers between devices with their start and end apart: 11, of which 7 were waited for; matrix products, arithmetic and copies ran while one was open for 0% of the time, Pallas kernels for 1%

profile of v1, /device:TPU:0, one launch (start us, length us, event | category | flops | bytes accessed | tf_op | source)
XLA Modules:
  0.0 45.6 jit_solution(2593674026742968616)
XLA Ops:
  2.6 2.5 %attend.1 = (f32[40,1536]{1,0:T(8,128)S(1)}, f32[40,1536]{1,0:T(8,128)S(1)}, f32[1,768]{1,0:T(1,128)S(1)}, s32[1,256]{1,0:T(1,128)S(1)}, s32[80,128]{1,0:T(8,128)S(1)}, /*index=5*/s32[1,128]{1,0:T(1,128)S(1)}) custom-call(s32[1]{0:T(128)S(6)} %copy.21.cache_len, s32[1]{0:T(128)S(6)} %copy.22.sink, s32[1]{0:T(128)S(6)} %copy.23.window, s32[8]{0:T(128)} %lengths_ref.1, ...), custom_call_target="tpu_custom_call" | custom-call | tf_op jit(solution)/shard_map/attend/pallas_call | solution.py:350
  5.1 0.0 copy-start
  5.2 0.5 %collective-permute-start = (bf16[40,1536]{1,0:T(8,128)(2,1)S(1)}, bf16[40,1536]{1,0:T(8,128)(2,1)S(1)}, u32[]{:S(2)}, u32[]{:S(2)}) collective-permute-start(bf16[40,1536]{1,0:T(8,128)(2,1)S(1)} %convert_element_type.27), channel_id=1, source_target_pairs={{0,1},{1,0},{2,3},{3,2},{4,5},{5,4},{6,7},{7,6},{8,9},{9,8},{10,11... | collective-permute-start | bytes 368648 | tf_op jit(solution)/shard_map/ppermute | solution.py:25
  5.7 1.0 %collective-permute-done = bf16[40,1536]{1,0:T(8,128)(2,1)S(1)} collective-permute-done((bf16[40,1536]{1,0:T(8,128)(2,1)S(1)}, bf16[40,1536]{1,0:T(8,128)(2,1)S(1)}, u32[]{:S(2)}, u32[]{:S(2)}) %collective-permute-start) | collective-permute-done | bytes 122912 | tf_op jit(solution)/shard_map/ppermute | solution.py:25
  6.7 2.9 %collective-permute-start.1 = (bf16[40,768]{1,0:T(8,128)(2,1)S(1)}, bf16[40,768]{1,0:T(8,128)(2,1)S(1)}, u32[]{:S(2)}, u32[]{:S(2)}) collective-permute-start(bf16[40,768]{1,0:T(8,128)(2,1)S(1)} %slice.53), channel_id=1, source_target_pairs={{0,2},{1,3},{2,0},{3,1},{4,6},{5,7},{6,4},{7,5},{8,10},{9,11},{10,... | collective-permute-start | bytes 184328 | tf_op jit(solution)/shard_map/ppermute | solution.py:25
  9.6 2.3 %collective-permute-done.1 = bf16[40,768]{1,0:T(8,128)(2,1)S(1)} collective-permute-done((bf16[40,768]{1,0:T(8,128)(2,1)S(1)}, bf16[40,768]{1,0:T(8,128)(2,1)S(1)}, u32[]{:S(2)}, u32[]{:S(2)}) %collective-permute-start.1) | collective-permute-done | bytes 61472 | tf_op jit(solution)/shard_map/ppermute | solution.py:25
  12.0 2.0 %collective-permute-start.4 = (bf16[1,32,768]{2,1,0:T(8,128)(2,1)S(1)}, bf16[1,32,768]{2,1,0:T(8,128)(2,1)S(1)}, u32[]{:S(2)}, u32[]{:S(2)}) collective-permute-start(bf16[1,32,768]{2,1,0:T(8,128)(2,1)S(1)} %get-tuple-element.23), channel_id=1, source_target_pairs={{0,8},{4,12},{8,0},{12,4},{16,24},{20,28},{24,16},{28,20},{1,9},{5... | collective-permute-start | bytes 147464 | tf_op jit(solution)/shard_map/ppermute | solution.py:25
  14.0 2.6 %collective-permute-start.3 = (bf16[1,32,768]{2,1,0:T(8,128)(2,1)S(1)}, bf16[1,32,768]{2,1,0:T(8,128)(2,1)S(1)}, u32[]{:S(2)}, u32[]{:S(2)}) collective-permute-start(bf16[1,32,768]{2,1,0:T(8,128)(2,1)S(1)} %get-tuple-element.23), channel_id=1, source_target_pairs={{0,16},{4,20},{8,24},{12,28},{16,0},{20,4},{24,8},{28,12},{1,17},{... | collective-permute-start | bytes 147464 | tf_op jit(solution)/shard_map/ppermute | solution.py:25
  16.6 0.0 copy-done
  16.6 0.1 dynamic-slice_bitcast_fusion
  16.7 0.1 collective-permute-start.8
  16.8 1.6 %collective-permute-start.5 = (bf16[1,32,768]{2,1,0:T(8,128)(2,1)S(1)}, bf16[1,32,768]{2,1,0:T(8,128)(2,1)S(1)}, u32[]{:S(2)}, u32[]{:S(2)}) collective-permute-start(bf16[1,32,768]{2,1,0:T(8,128)(2,1)S(1)} %get-tuple-element.23), channel_id=1, source_target_pairs={{0,4},{4,0},{8,12},{12,8},{16,20},{20,16},{24,28},{28,24},{1,5},{5... | collective-permute-start | bytes 147464 | tf_op jit(solution)/shard_map/ppermute | solution.py:25
  18.3 0.2 collective-permute-start.2
  18.6 0.0 collective-permute-done.4
  18.6 1.0 %collective-permute-done.3 = bf16[1,32,768]{2,1,0:T(8,128)(2,1)S(1)} collective-permute-done((bf16[1,32,768]{2,1,0:T(8,128)(2,1)S(1)}, bf16[1,32,768]{2,1,0:T(8,128)(2,1)S(1)}, u32[]{:S(2)}, u32[]{:S(2)}) %collective-permute-start.3) | collective-permute-done | bytes 49184 | tf_op jit(solution)/shard_map/ppermute | solution.py:25
  19.6 1.6 %collective-permute-start.7 = (bf16[2,32,768]{2,1,0:T(8,128)(2,1)S(1)}, bf16[2,32,768]{2,1,0:T(8,128)(2,1)S(1)}, u32[]{:S(2)}, u32[]{:S(2)}) collective-permute-start(bf16[2,32,768]{2,1,0:T(8,128)(2,1)S(1)} %pad_maximum_fusion), channel_id=1, source_target_pairs={{0,4},{4,0},{8,12},{12,8},{16,20},{20,16},{24,28},{28,24},{1,5},{5... | collective-permute-start | bytes 294920 | tf_op jit(solution)/shard_map/ppermute | solution.py:25
  21.1 3.1 %collective-permute-done.2 = bf16[1,32,768]{2,1,0:T(8,128)(2,1)S(1)} collective-permute-done((bf16[1,32,768]{2,1,0:T(8,128)(2,1)S(1)}, bf16[1,32,768]{2,1,0:T(8,128)(2,1)S(1)}, u32[]{:S(2)}, u32[]{:S(2)}) %collective-permute-start.2) | collective-permute-done | bytes 49184 | tf_op jit(solution)/shard_map/ppermute | solution.py:25
  24.2 0.5 %collective-permute-start.6 = (bf16[1,32,768]{2,1,0:T(8,128)(2,1)S(1)}, bf16[1,32,768]{2,1,0:T(8,128)(2,1)S(1)}, u32[]{:S(2)}, u32[]{:S(2)}) collective-permute-start(bf16[1,32,768]{2,1,0:T(8,128)(2,1)S(1)} %collective-permute-done.2), channel_id=1, source_target_pairs={{0,4},{4,0},{8,12},{12,8},{16,20},{20,16},{24,28},{28,24},{1,5},{5... | collective-permute-start | bytes 147464 | tf_op jit(solution)/shard_map/ppermute | solution.py:25
  24.8 0.0 collective-permute-done.5
  24.8 3.5 %collective-permute-done.6 = bf16[1,32,768]{2,1,0:T(8,128)(2,1)S(1)} collective-permute-done((bf16[1,32,768]{2,1,0:T(8,128)(2,1)S(1)}, bf16[1,32,768]{2,1,0:T(8,128)(2,1)S(1)}, u32[]{:S(2)}, u32[]{:S(2)}) %collective-permute-start.6) | collective-permute-done | bytes 49184 | tf_op jit(solution)/shard_map/ppermute | solution.py:25
  28.3 0.0 collective-permute-done.7
  28.3 0.0 collective-permute-done.8.got_ref
  28.3 0.9 %logits.1 = (f32[2,40,1152]{2,1,0:T(8,128)S(1)}, f32[2,40,1152]{2,1,0:T(8,128)S(1)}) custom-call(s32[1,256]{1,0:T(1,128)S(1)} %get-tuple-element.13.index_ref, bf16[8,32,768]{2,1,0:T(8,128)(2,1)S(1)} %constant_dynamic-update-slice_fusion.rows_ref, f32[1,768]{1,0:T(1,128)S(1)} %get-tuple-element.17.gain_ref, bf16[2,1024,384]{2,1,0:T(8,128)(2,1)S(1)} %copy-done, ...), custom_call_target="tpu_custom_call" | custom-call | flops 1 | bytes 1 | tf_op jit(solution)/shard_map/logits/pallas_call | solution.py:417
  29.3 1.6 %collective-permute-start.10 = (bf16[40,1152]{1,0:T(8,128)(2,1)S(1)}, bf16[40,1152]{1,0:T(8,128)(2,1)S(1)}, u32[]{:S(2)}, u32[]{:S(2)}) collective-permute-start(bf16[40,1152]{1,0:T(8,128)(2,1)S(1)} %get-tuple-element.24), channel_id=1, source_target_pairs={{0,2},{1,3},{2,0},{3,1},{4,6},{5,7},{6,4},{7,5},{8,10},{9,11},{10,... | collective-permute-start | bytes 276488 | tf_op jit(solution)/shard_map/ppermute | solution.py:25
  30.9 0.5 %collective-permute-start.9 = (bf16[40,1152]{1,0:T(8,128)(2,1)S(1)}, bf16[40,1152]{1,0:T(8,128)(2,1)S(1)}, u32[]{:S(2)}, u32[]{:S(2)}) collective-permute-start(bf16[40,1152]{1,0:T(8,128)(2,1)S(1)} %get-tuple-element.25), channel_id=1, source_target_pairs={{0,2},{1,3},{2,0},{3,1},{4,6},{5,7},{6,4},{7,5},{8,10},{9,11},{10,... | collective-permute-start | bytes 276488 | tf_op jit(solution)/shard_map/ppermute | solution.py:25
  31.4 2.5 %collective-permute-done.10 = bf16[40,1152]{1,0:T(8,128)(2,1)S(1)} collective-permute-done((bf16[40,1152]{1,0:T(8,128)(2,1)S(1)}, bf16[40,1152]{1,0:T(8,128)(2,1)S(1)}, u32[]{:S(2)}, u32[]{:S(2)}) %collective-permute-start.10) | collective-permute-done | bytes 92192 | tf_op jit(solution)/shard_map/ppermute | solution.py:25
  34.0 0.3 lse.2.refs_0_
  34.3 1.2 %collective-permute-done.9 = bf16[40,1152]{1,0:T(8,128)(2,1)S(1)} collective-permute-done((bf16[40,1152]{1,0:T(8,128)(2,1)S(1)}, bf16[40,1152]{1,0:T(8,128)(2,1)S(1)}, u32[]{:S(2)}, u32[]{:S(2)}) %collective-permute-start.9) | collective-permute-done | bytes 92192 | tf_op jit(solution)/shard_map/ppermute | solution.py:25
  35.5 0.4 lse.3
  35.9 8.9 %all_to_all.5.stats_ref = f32[32,2,128]{2,1,0:T(2,128)S(1)} all-to-all(f32[32,2,128]{2,1,0:T(2,128)S(1)} %lse.3), channel_id=1, replica_groups=mesh['req'=8,'tp'=4] {'req','tp'}, dimensions={0} | all-to-all | bytes 65536 | tf_op jit(solution)/shard_map/all_to_all | solution.py:451
  44.8 0.7 %final.1 = (f32[1,8]{1,0:T(1,128)}, f32[1,2]{1,0:T(1,128)}) custom-call(s32[1,128]{1,0:T(1,128)S(1)} %get-tuple-element.12.span_ref, f32[32,2,128]{2,1,0:T(2,128)S(1)} %all_to_all.5.stats_ref), custom_call_target="tpu_custom_call" | custom-call | tf_op jit(solution)/shard_map/final/pallas_call | solution.py:452
  (18 shorter events, 0.2 us)
Async XLA Ops:
  5.1 11.5 %copy-start = (bf16[2,1024,384]{2,1,0:T(8,128)(2,1)S(1)}, bf16[2,1024,384]{2,1,0:T(8,128)(2,1)}, u32[]{:S(2)}) copy-start(bf16[2,1024,384]{2,1,0:T(8,128)(2,1)} %head_ref.1) | copy-start | bytes 4718596
  5.2 1.5 %collective-permute-start = (bf16[40,1536]{1,0:T(8,128)(2,1)S(1)}, bf16[40,1536]{1,0:T(8,128)(2,1)S(1)}, u32[]{:S(2)}, u32[]{:S(2)}) collective-permute-start(bf16[40,1536]{1,0:T(8,128)(2,1)S(1)} %convert_element_type.27), channel_id=1, source_target_pairs={{0,1},{1,0},{2,3},{3,2},{4,5},{5,4},{6,7},{7,6},{8,9},{9,8},{10,11... | collective-permute-start | bytes 368648 | tf_op jit(solution)/shard_map/ppermute | solution.py:25
  6.7 5.3 %collective-permute-start.1 = (bf16[40,768]{1,0:T(8,128)(2,1)S(1)}, bf16[40,768]{1,0:T(8,128)(2,1)S(1)}, u32[]{:S(2)}, u32[]{:S(2)}) collective-permute-start(bf16[40,768]{1,0:T(8,128)(2,1)S(1)} %slice.53), channel_id=1, source_target_pairs={{0,2},{1,3},{2,0},{3,1},{4,6},{5,7},{6,4},{7,5},{8,10},{9,11},{10,... | collective-permute-start | bytes 184328 | tf_op jit(solution)/shard_map/ppermute | solution.py:25
  12.0 6.6 %collective-permute-start.4 = (bf16[1,32,768]{2,1,0:T(8,128)(2,1)S(1)}, bf16[1,32,768]{2,1,0:T(8,128)(2,1)S(1)}, u32[]{:S(2)}, u32[]{:S(2)}) collective-permute-start(bf16[1,32,768]{2,1,0:T(8,128)(2,1)S(1)} %get-tuple-element.23), channel_id=1, source_target_pairs={{0,8},{4,12},{8,0},{12,4},{16,24},{20,28},{24,16},{28,20},{1,9},{5... | collective-permute-start | bytes 147464 | tf_op jit(solution)/shard_map/ppermute | solution.py:25
  14.0 5.5 %collective-permute-start.3 = (bf16[1,32,768]{2,1,0:T(8,128)(2,1)S(1)}, bf16[1,32,768]{2,1,0:T(8,128)(2,1)S(1)}, u32[]{:S(2)}, u32[]{:S(2)}) collective-permute-start(bf16[1,32,768]{2,1,0:T(8,128)(2,1)S(1)} %get-tuple-element.23), channel_id=1, source_target_pairs={{0,16},{4,20},{8,24},{12,28},{16,0},{20,4},{24,8},{28,12},{1,17},{... | collective-permute-start | bytes 147464 | tf_op jit(solution)/shard_map/ppermute | solution.py:25
  16.7 11.6 %collective-permute-start.8 = (bf16[1024,384]{1,0:T(8,128)(2,1)S(1)}, bf16[1024,384]{1,0:T(8,128)(2,1)S(1)}, u32[]{:S(2)}, u32[]{:S(2)}) collective-permute-start(bf16[1024,384]{1,0:T(8,128)(2,1)S(1)} %dynamic-slice_bitcast_fusion), channel_id=1, source_target_pairs={{0,1},{1,0},{2,3},{3,2},{4,5},{5,4},{6,7},{7,6},{8,9},{9,8},{10,11... | collective-permute-start | bytes 2359304 | tf_op jit(solution)/shard_map/ppermute | solution.py:25
  16.8 8.0 %collective-permute-start.5 = (bf16[1,32,768]{2,1,0:T(8,128)(2,1)S(1)}, bf16[1,32,768]{2,1,0:T(8,128)(2,1)S(1)}, u32[]{:S(2)}, u32[]{:S(2)}) collective-permute-start(bf16[1,32,768]{2,1,0:T(8,128)(2,1)S(1)} %get-tuple-element.23), channel_id=1, source_target_pairs={{0,4},{4,0},{8,12},{12,8},{16,20},{20,16},{24,28},{28,24},{1,5},{5... | collective-permute-start | bytes 147464 | tf_op jit(solution)/shard_map/ppermute | solution.py:25
  18.3 5.9 %collective-permute-start.2 = (bf16[1,32,768]{2,1,0:T(8,128)(2,1)S(1)}, bf16[1,32,768]{2,1,0:T(8,128)(2,1)S(1)}, u32[]{:S(2)}, u32[]{:S(2)}) collective-permute-start(bf16[1,32,768]{2,1,0:T(8,128)(2,1)S(1)} %get-tuple-element.23), channel_id=1, source_target_pairs={{0,24},{4,28},{8,16},{12,20},{16,8},{20,12},{24,0},{28,4},{1,25},{... | collective-permute-start | bytes 147464 | tf_op jit(solution)/shard_map/ppermute | solution.py:25
  19.6 8.8 %collective-permute-start.7 = (bf16[2,32,768]{2,1,0:T(8,128)(2,1)S(1)}, bf16[2,32,768]{2,1,0:T(8,128)(2,1)S(1)}, u32[]{:S(2)}, u32[]{:S(2)}) collective-permute-start(bf16[2,32,768]{2,1,0:T(8,128)(2,1)S(1)} %pad_maximum_fusion), channel_id=1, source_target_pairs={{0,4},{4,0},{8,12},{12,8},{16,20},{20,16},{24,28},{28,24},{1,5},{5... | collective-permute-start | bytes 294920 | tf_op jit(solution)/shard_map/ppermute | solution.py:25
  24.2 4.1 %collective-permute-start.6 = (bf16[1,32,768]{2,1,0:T(8,128)(2,1)S(1)}, bf16[1,32,768]{2,1,0:T(8,128)(2,1)S(1)}, u32[]{:S(2)}, u32[]{:S(2)}) collective-permute-start(bf16[1,32,768]{2,1,0:T(8,128)(2,1)S(1)} %collective-permute-done.2), channel_id=1, source_target_pairs={{0,4},{4,0},{8,12},{12,8},{16,20},{20,16},{24,28},{28,24},{1,5},{5... | collective-permute-start | bytes 147464 | tf_op jit(solution)/shard_map/ppermute | solution.py:25
  29.3 4.6 %collective-permute-start.10 = (bf16[40,1152]{1,0:T(8,128)(2,1)S(1)}, bf16[40,1152]{1,0:T(8,128)(2,1)S(1)}, u32[]{:S(2)}, u32[]{:S(2)}) collective-permute-start(bf16[40,1152]{1,0:T(8,128)(2,1)S(1)} %get-tuple-element.24), channel_id=1, source_target_pairs={{0,2},{1,3},{2,0},{3,1},{4,6},{5,7},{6,4},{7,5},{8,10},{9,11},{10,... | collective-permute-start | bytes 276488 | tf_op jit(solution)/shard_map/ppermute | solution.py:25
  30.9 4.6 %collective-permute-start.9 = (bf16[40,1152]{1,0:T(8,128)(2,1)S(1)}, bf16[40,1152]{1,0:T(8,128)(2,1)S(1)}, u32[]{:S(2)}, u32[]{:S(2)}) collective-permute-start(bf16[40,1152]{1,0:T(8,128)(2,1)S(1)} %get-tuple-element.25), channel_id=1, source_target_pairs={{0,2},{1,3},{2,0},{3,1},{4,6},{5,7},{6,4},{7,5},{8,10},{9,11},{10,... | collective-permute-start | bytes 276488 | tf_op jit(solution)/shard_map/ppermute | solution.py:25
